TPU v7x, 32 devices: a whole 2x2x4 slice. The times are simulated.
32 devices in a mesh: rep: 2 (over y), expert: 16 (over z, x, core).
Axes of the slice: x: 2, y: 2, z: 4, core: 2. Of those that a mesh axis runs over, the one named last changes fastest.
Arguments:
- tokens: bfloat16 [2048, 4096], P('expert', 'rep')
- norm_gain: float32 [4096], P('rep'), may hold values from 0.25 to 1.75
- gate_weights: float32 [2048, 8], P('expert'), may hold values from 0.1 to 0.6
- exit_flags: int32 [2048], P('expert'), may hold values from 0 to 1, as said below
- routes: int32 [2048, 8], P('expert'), may hold values from 0 to 31, as said below
- next_device: int32 [2048], P('expert'), may hold values from 0 to 15, as said below
- up_weight: bfloat16 [32, 4096, 1024], P('expert', 'rep'), may hold values from -0.09375 to 0.09375
- down_weight: bfloat16 [32, 1024, 4096], P('expert', None, 'rep'), may hold values from -0.1875 to 0.1875
Outputs:
- handed: float32 [1024, 4096], P('expert', 'rep')
Inputs may be any that keep to these rules, and one draw needn't show every extreme that they name: `exit_flags`: one block of 128 rows holds at most 64 live rows; some block holds exactly 64. `routes`: each row names 8 different experts. Among the live rows of one block, every expert is named the same number of times up to one, so at most 16 times; a block with 64 live rows names every expert exactly 16 times. `next_device`: among the live rows of one block, every value is named the same number of times up to one, so at most 4 times.
All inputs are finite; a program needn't handle non-finite values.
Results may differ from a plain program's by a relative error of at most 0.0017.
Values may be sent and summed in bfloat16 or wider, within the bound.
A program may use at most 64 MiB of HBM per device.

v0:
```python
import jax
import jax.numpy as jnp
from jax import lax
from jax.sharding import PartitionSpec as P

F32 = jnp.float32
BF16 = jnp.bfloat16


def lower_ones(n):
    i = jnp.arange(n)
    return (i[:, None] > i[None, :]).astype(BF16)


def rep_sum(value, reps):
    if reps != 2:
        return lax.psum(value, "rep")
    return value + lax.ppermute(value.astype(BF16), "rep", [(0, 1), (1, 0)]).astype(F32)


def expert_reduce(value):
    return lax.psum_scatter(value, "expert", scatter_dimension=0, tiled=False)


def per_device(
    tokens, norm_gain, gate_weights, exit_flags, routes, next_device, up_weight, down_weight
):
    row_count, width = tokens.shape
    owners = lax.axis_size("expert")
    reps = lax.axis_size("rep")
    local_experts = up_weight.shape[0]
    top = routes.shape[1]
    experts_all = local_experts * owners
    most_live = row_count // 2
    cap = top * most_live // experts_all
    hand_cap = (most_live + owners - 1) // owners
    packed_rows = owners * hand_cap

    live = exit_flags == 0
    dest_hot = (
        (next_device[:, None] == jnp.arange(owners)[None, :]) & live[:, None]
    ).astype(BF16)
    before = jnp.dot(lower_ones(row_count), dest_hot, preferred_element_type=F32)
    pos = jnp.sum(before * dest_hot.astype(F32), axis=1).astype(jnp.int32)
    slot = jnp.where(live, next_device * hand_cap + pos, packed_rows)
    pick = slot[None, :] == jnp.arange(packed_rows)[:, None]
    packed = jnp.dot(pick.astype(BF16), tokens, preferred_element_type=F32)
    square = jnp.sum(packed * packed, axis=1)
    dense_gate = jnp.sum(
        jnp.where(
            routes[:, :, None] == jnp.arange(experts_all)[None, None, :],
            gate_weights[:, :, None],
            0.0,
        ),
        axis=1,
    )
    gate_packed = jnp.sum(
        jnp.where(pick[:, :, None], dense_gate[None, :, :], 0.0), axis=1
    )
    aux = jnp.concatenate([gate_packed, square[:, None]], axis=1)

    pieces = []
    rest = aux
    for _ in range(3):
        piece = lax.reduce_precision(rest, 8, 7)
        pieces.append(piece.astype(BF16))
        rest = rest - piece
    side = jnp.concatenate(pieces, axis=1)
    side = jnp.pad(side, ((0, 0), (0, -side.shape[1] % 128)))
    both = lax.all_gather(jnp.concatenate([packed.astype(BF16), side], axis=1), "expert")
    rows = both[:, :, :width]
    parts = both[:, :, width : width + 3 * aux.shape[1]].astype(F32)
    parts = parts.reshape(owners, packed_rows, 3, aux.shape[1])
    aux = parts[:, :, 0] + parts[:, :, 1] + parts[:, :, 2]
    rinv = lax.rsqrt(lax.psum(aux[:, :, experts_all], "rep") / (width * reps) + 1e-06)

    me = lax.axis_index("expert")
    gates = lax.dynamic_slice_in_dim(aux, me * local_experts, local_experts, axis=2)
    routed = (gates > 0).astype(BF16)
    place = jnp.einsum(
        "rt,ite->ire", lower_ones(packed_rows), routed, preferred_element_type=F32
    ).astype(jnp.int32)
    hot = (place[:, :, :, None] == jnp.arange(cap)) & (routed > 0)[:, :, :, None]
    hot = hot.reshape(owners, packed_rows, local_experts * cap)
    slots = jnp.einsum("irs,ird->isd", hot.astype(BF16), rows, preferred_element_type=F32)
    rinv_slot = jnp.sum(jnp.where(hot, rinv[:, :, None], 0.0), axis=1)
    normed = (slots * rinv_slot[:, :, None] * norm_gain).astype(BF16)
    normed = normed.reshape(owners, local_experts, cap, width)

    outs = []
    sums = []
    for e in range(local_experts):
        flat = normed[:, e].reshape(owners * cap, width)
        sums.append(
            rep_sum(jnp.dot(flat, up_weight[e], preferred_element_type=F32), reps)
        )
    for e in range(local_experts):
        act = jax.nn.silu(sums[e]).astype(BF16)
        out = jnp.dot(act, down_weight[e], preferred_element_type=F32).astype(BF16)
        outs.append(out.reshape(owners, cap, width))
    out = jnp.stack(outs, axis=1)
    out = out.reshape(owners * local_experts * cap, width)

    gate_slot = jnp.where(hot, jnp.repeat(gates, cap, axis=2), 0.0).astype(BF16)
    gate_slot = gate_slot.reshape(owners, owners, hand_cap, -1).transpose(1, 0, 2, 3)
    same = jnp.arange(owners)[:, None] == jnp.arange(owners)[None, :]
    weights = jnp.where(same[None, :, None, :, None], gate_slot[:, :, :, None, :], 0)
    weights = weights.reshape(owners * packed_rows, -1)
    mix = jnp.dot(weights, out, preferred_element_type=F32).astype(BF16)
    summed = expert_reduce(mix.reshape(owners, packed_rows, width))
    own = lax.dynamic_slice_in_dim(
        rows.reshape(owners, owners, hand_cap, width), me, 1, axis=1
    )[:, 0]
    return own.reshape(packed_rows, width).astype(F32) + summed.astype(F32)


def solution(mesh):
    in_specs = (
        P("expert", "rep"),
        P("rep"),
        P("expert", None),
        P("expert"),
        P("expert", None),
        P("expert"),
        P("expert", "rep", None),
        P("expert", None, "rep"),
    )
    return jax.shard_map(
        per_device, mesh=mesh, in_specs=in_specs, out_specs=P("expert", "rep"), check_vma=False
    )
```

profile of v0, /device:TPU:0, one launch (start us, length us, event | category | flops | bytes accessed | tf_op | source)
XLA Modules:
  0.0 200.8 jit_solution(8220704178080550687)
XLA Ops:
  6.5 0.7 broadcast_compare_fusion.1
  7.3 0.9 fusion.19
  8.1 0.7 add_select_fusion
  9.3 0.7 select_reduce_fusion.2
  10.0 0.3 select_reduce_fusion.1
  10.5 0.7 pad_maximum_fusion.1
  11.4 54.7 %all-gather.3.cloned.1.call-done = bf16[1024,2176]{1,0:T(8,128)(2,1)} async-done(((bf16[64,2176]{1,0:T(8,128)(2,1)}), bf16[1024,2176]{1,0:T(8,128)(2,1)}) %all-gather.3.cloned.1.call-update) | async-done | bytes 4456464 | tf_op jit(solution)/shard_map/all_gather | solution.py:70
  66.1 1.0 slice_convert_fusion
  67.1 0.4 copy.51
  67.7 5.0 %psum.7 = f32[16,64]{1,0:T(8,128)S(1)} all-reduce(f32[16,64]{1,0:T(8,128)S(1)} %slice_bitcast_fusion), channel_id=1, replica_groups=mesh['rep'=2,'expert'=16] {'rep'}, use_global_device_ids=true, to_apply=%region_4.5 | all-reduce | flops 1024 | bytes 8192 | tf_op jit(solution)/shard_map/psum | solution.py:75
  73.2 0.3 select_reduce_fusion
  73.6 0.8 copy.59
  74.5 0.4 copy.55
  75.2 1.4 broadcast_in_dim.110
  77.0 0.7 copy.58
  78.0 3.3 %multiply_convert_fusion = bf16[16,32,2048]{2,1,0:T(8,128)(2,1)S(1)} fusion(f32[2048]{0:T(1024)S(1)} %copy-done.1, f32[16,32]{1,0:T(8,128)S(1)} %copy.61, pred[16,64,32]{1,2,0:T(32,128)(4,1)S(1)} %copy.59, s32[16,64,32]{1,2,0:T(8,128)S(1)} %copy.58, s32[32]{0:T(128)S(1)} %eq.119, bf16[16,64,2176]{2,1,0:T(8,128)(2,1)} %bitcast.71), kind=kOutput, calls=%fused_computation.12 | convolution fusion | flops 137428992 | bytes 6465664 | tf_op jit(solution)/shard_map/irs,ird->isd/dot_general | solution.py:85
  81.4 4.7 %fusion.47 = (bf16[256,1024]{1,0:T(8,128)(2,1)S(1)}, f32[256,1024]{1,0:T(8,128)}) fusion(bf16[256,2048]{1,0:T(8,128)(2,1)S(1)} %bitcast.80, bf16[2,2048,1024]{2,1,0:T(8,128)(2,1)} %param.14), kind=kOutput, calls=%fused_computation.80 | convolution fusion | flops 1074003968 | bytes 6815744 | tf_op jit(solution)/shard_map/dot_general | solution.py:95
  86.1 2.4 %fusion.48 = (bf16[256,1024]{1,0:T(8,128)(2,1)}, f32[256,1024]{1,0:T(8,128)}) fusion(bf16[256,2048]{1,0:T(8,128)(2,1)S(1)} %bitcast.79, bf16[2,2048,1024]{2,1,0:T(8,128)(2,1)S(1)} %bitcast.85), kind=kOutput, calls=%fused_computation.81 | convolution fusion | flops 1074003968 | bytes 6815744 | tf_op jit(solution)/shard_map/dot_general | solution.py:95
  88.5 1.5 collective-permute-start
  90.3 0.6 collective-permute-start.1
  90.9 2.4 %broadcast_select_fusion = bf16[16,16,4,16,32]{4,3,2,1,0:T(8,128)(2,1)} fusion(pred[16,16]{1,0:T(8,128)(4,1)S(1)} %iota_compare_fusion.7, bf16[16,16,4,32]{3,2,1,0:T(4,128)(2,1)S(1)} %copy.57), kind=kLoop, calls=%fused_computation.13 | loop fusion | flops 524288 | bytes 1114368 | tf_op jit(solution)/shard_map/jit(_where)/select_n | solution.py:107
  93.3 5.9 %select_n.49 = bf16[1024,512]{1,0:T(8,128)(2,1)S(1)} reshape(bf16[16,16,4,16,32]{4,3,2,1,0:T(8,128)(2,1)} %broadcast_select_fusion) | data formatting | bytes 2097152 | tf_op jit(solution)/shard_map/jit(_where)/select_n | solution.py:107
  99.3 4.4 %collective-permute-done = bf16[256,1024]{1,0:T(8,128)(2,1)} collective-permute-done((bf16[256,1024]{1,0:T(8,128)(2,1)}, bf16[256,1024]{1,0:T(8,128)(2,1)}, u32[]{:S(2)}, u32[]{:S(2)}) %collective-permute-start) | collective-permute-done | bytes 524320 | tf_op jit(solution)/shard_map/ppermute | solution.py:18
  103.7 4.0 %fusion.12 = bf16[256,2048]{1,0:T(8,128)(2,1)S(1)} fusion(bf16[2,1024,2048]{2,1,0:T(8,128)(2,1)} %param.15, f32[256,1024]{1,0:T(8,128)} %get-tuple-element.18, bf16[256,1024]{1,0:T(8,128)(2,1)} %collective-permute-done), kind=kOutput, calls=%fused_computation.15 | convolution fusion | flops 1076101120 | bytes 6815744 | tf_op jit(solution)/shard_map/dot_general | solution.py:99
  107.7 5.1 %collective-permute-done.1 = bf16[256,1024]{1,0:T(8,128)(2,1)S(1)} collective-permute-done((bf16[256,1024]{1,0:T(8,128)(2,1)S(1)}, bf16[256,1024]{1,0:T(8,128)(2,1)S(1)}, u32[]{:S(2)}, u32[]{:S(2)}) %collective-permute-start.1) | collective-permute-done | bytes 524320 | tf_op jit(solution)/shard_map/ppermute | solution.py:18
  112.9 3.5 %fusion.15 = bf16[256,2048]{1,0:T(8,128)(2,1)S(1)} fusion(bf16[2,1024,2048]{2,1,0:T(8,128)(2,1)} %param.15, f32[256,1024]{1,0:T(8,128)S(1)} %copy-done.2, bf16[256,1024]{1,0:T(8,128)(2,1)S(1)} %collective-permute-done.1), kind=kOutput, calls=%fused_computation.16 | convolution fusion | flops 1076101120 | bytes 6815744 | tf_op jit(solution)/shard_map/dot_general | solution.py:99
  116.6 4.3 %convolution_convert_fusion = bf16[1024,2048]{1,0:T(8,128)(2,1)} fusion(bf16[1024,512]{1,0:T(8,128)(2,1)S(1)} %select_n.49, bf16[512,2048]{1,0:T(8,128)(2,1)S(1)} %bitcast.77), kind=kOutput, calls=%fused_computation.14 | convolution fusion | flops 2149580800 | bytes 7340032 | tf_op jit(solution)/shard_map/dot_general | solution.py:109
  121.0 4.7 %slice.48 = bf16[16,64,2048]{2,1,0:T(8,128)(2,1)} slice(bf16[16,64,2176]{2,1,0:T(8,128)(2,1)} %bitcast.72), slice={[0:16], [0:64], [0:2048]} | slice | bytes 8388608 | tf_op jit(solution)/shard_map/slice | solution.py:71
  125.7 7.3 %reshape.94 = bf16[16,16,4,2048]{3,2,1,0:T(4,128)(2,1)} reshape(bf16[16,64,2048]{2,1,0:T(8,128)(2,1)} %slice.48) | data formatting | bytes 8388608 | tf_op jit(solution)/shard_map/reshape | solution.py:112
  133.1 1.0 dynamic-slice_convert_fusion
  134.3 57.8 %reduce-scatter.2.cloned.1.call-done = bf16[1,64,2048]{2,1,0:T(8,128)(2,1)} async-done(((bf16[16,64,2048]{2,1,0:T(8,128)(2,1)}), bf16[1,64,2048]{2,1,0:T(8,128)(2,1)}) %reduce-scatter.2.cloned.1.call-update) | async-done | bytes 262160 | tf_op jit(solution)/shard_map/reduce_scatter | solution.py:22
  192.1 1.8 convert_add_fusion
  (43 shorter events, 3.2 us)
Async XLA Ops:
  6.5 2.3 %copy-start = (bf16[128,2048]{1,0:T(8,128)(2,1)S(1)}, bf16[128,2048]{1,0:T(8,128)(2,1)}, u32[]{:S(2)}) copy-start(bf16[128,2048]{1,0:T(8,128)(2,1)} %param.8) | copy-start | bytes 1572868
  6.5 59.6 %all-gather.3.cloned.1.call-start = ((), (), s32[]{:S(2)}) async-start(), calls=%async_computation.2 | async-start | bytes 4734976 | tf_op jit(solution)/shard_map/all_gather | solution.py:70
  11.3 180.8 %reduce-scatter.2.cloned.1.call-start = ((), (), s32[]{:S(2)}) async-start(), calls=%async_computation.1 | async-start | bytes 4456448 | tf_op jit(solution)/shard_map/reduce_scatter | solution.py:22
  67.6 10.4 %copy-start.1 = (f32[2048]{0:T(1024)S(1)}, f32[2048]{0:T(1024)}, u32[]{:S(2)}) copy-start(f32[2048]{0:T(1024)} %param.9) | copy-start | bytes 24580
  78.0 8.1 %slice-start = ((s8[8388608]{0:T(1024)(128)(4,1)}), s8[4194304]{0:T(1024)(128)(4,1)S(1)}, s32[]{:S(2)}) async-start(s8[8388608]{0:T(1024)(128)(4,1)} %bitcast.84), calls=%async_computation.3 | async-start | bytes 8388608
  81.3 4.8 %slice-start.1 = ((s8[8388608]{0:T(1024)(128)(4,1)}), s8[4194304]{0:T(1024)(128)(4,1)S(1)}, s32[]{:S(2)}) async-start(s8[8388608]{0:T(1024)(128)(4,1)} %bitcast.84), calls=%async_computation.4 | async-start | bytes 8388608
  88.5 15.2 %collective-permute-start = (bf16[256,1024]{1,0:T(8,128)(2,1)}, bf16[256,1024]{1,0:T(8,128)(2,1)}, u32[]{:S(2)}, u32[]{:S(2)}) collective-permute-start(bf16[256,1024]{1,0:T(8,128)(2,1)} %get-tuple-element.17), channel_id=1, source_target_pairs={{0,16},{16,0},{1,17},{17,1},{2,18},{18,2},{3,19},{19,3},{4,20},{20... | collective-permute-start | bytes 1572872 | tf_op jit(solution)/shard_map/ppermute | solution.py:18
  90.3 22.6 %collective-permute-start.1 = (bf16[256,1024]{1,0:T(8,128)(2,1)S(1)}, bf16[256,1024]{1,0:T(8,128)(2,1)S(1)}, u32[]{:S(2)}, u32[]{:S(2)}) collective-permute-start(bf16[256,1024]{1,0:T(8,128)(2,1)S(1)} %get-tuple-element.15), channel_id=1, source_target_pairs={{0,16},{16,0},{1,17},{17,1},{2,18},{18,2},{3,19},{19,3},{4,20},{20... | collective-permute-start | bytes 1572872 | tf_op jit(solution)/shard_map/ppermute | solution.py:18
  103.7 9.2 %copy-start.2 = (f32[256,1024]{1,0:T(8,128)S(1)}, f32[256,1024]{1,0:T(8,128)}, u32[]{:S(2)}) copy-start(f32[256,1024]{1,0:T(8,128)} %get-tuple-element.16) | copy-start | bytes 3145732
Sparse Core Ops, SparseCore 0:
  11.4 54.6 all-gather.2
  121.1 70.9 reduce-scatter.1
where the time goes:
time: 201 us
  waiting for transfers between devices  122 us (61%)
  local copies, waits for them, and re-layouts  23.8 us (12%)
  matrix products  23.6 us (12%)
  between operations  13.7 us (7%)
  other arithmetic  10.4 us (5%)
  blocking collectives  5.01 us (2%)
  starting transfers between devices  2.14 us (1%)
    reduce_scatter x1, waiting for transfers between devices, expert_reduce(): return lax.psum_scatter(value, 'expert', scatter_dimension=0, tiled=False)  57.8 us
    all_gather x1, waiting for transfers between devices, per_device(): lax.all_gather(jnp.concatenate([packed.astype(BF16), side], axis=1), 'exp...  54.7 us
    ppermute x2, waiting for transfers between devices, rep_sum(): lax.ppermute(value.astype(BF16), 'rep', [(0, 1), (1, 0)]).astype(F32)  9.59 us
    dot_general x2, matrix products, per_device(): out = jnp.dot(act, down_weight[e], preferred_element_type=F32).astype(BF16)  7.56 us
    reshape x1, local copies, waits for them, and re-layouts, per_device(): rows.reshape(owners, owners, hand_cap, width)  7.34 us
    dot_general x2, matrix products, per_device(): jnp.dot(flat, up_weight[e], preferred_element_type=F32)  7.08 us
    select_n x1, local copies, waits for them, and re-layouts, per_device(): jnp.where(same[None, :, None, :, None], gate_slot[:, :, :, None, :], 0)  5.93 us
    psum x1, blocking collectives, per_device(): lax.psum(aux[:, :, experts_all], 'rep') / (width * reps) + 1e-06  5.01 us
  transfers between devices with their start and end apart: 4, of which 4 were waited for; matrix products, arithmetic and copies ran while one was open for 13% of the time, Pallas kernels for 0%

commit v1 on v0

--- a/solution.py
+++ b/solution.py
@@ -1,6 +1,10 @@
+import functools
+
 import jax
 import jax.numpy as jnp
 from jax import lax
+from jax.experimental import pallas as pl
+from jax.experimental.pallas import tpu as pltpu
 from jax.sharding import PartitionSpec as P
 
 F32 = jnp.float32
@@ -18,8 +22,232 @@
     return value + lax.ppermute(value.astype(BF16), "rep", [(0, 1), (1, 0)]).astype(F32)
 
 
+Z, X, C = 4, 2, 2
+MESH = pl.DeviceIdType.MESH
+
+
+def place_of():
+    me = lax.axis_index("expert")
+    return lax.axis_index("rep"), me // (X * C), me // C % X, me % C
+
+
+def index_of(z, x, c):
+    return (z * X + x) * C + c
+
+
+def greet(rep, z, x, c):
+    barrier = pltpu.get_barrier_semaphore()
+
+    def signal(where):
+        pl.semaphore_signal(barrier, inc=1, device_id=(rep, where), device_id_type=MESH)
+
+    signal(index_of(z, 1 - x, c))
+    signal(index_of(z, x, 1 - c))
+    pl.when(z > 0)(lambda: signal(index_of(z - 1, x, c)))
+    pl.when(z < Z - 1)(lambda: signal(index_of(z + 1, x, c)))
+    inner = (z > 0) & (z < Z - 1)
+    pl.when(inner)(lambda: pl.semaphore_wait(barrier, 4))
+    pl.when(jnp.logical_not(inner))(lambda: pl.semaphore_wait(barrier, 3))
+
+
+def gather_kernel(own, out, local_sem, send, recv):
+    rep, z, x, c = place_of()
+    mine = index_of(z, x, c)
+    greet(rep, z, x, c)
+    local = pltpu.make_async_copy(own, out.at[mine], local_sem)
+    local.start()
+
+    def copy(block, sem, where, source=None):
+        return pltpu.make_async_remote_copy(
+            src_ref=out.at[block] if source is None else source,
+            dst_ref=out.at[block],
+            send_sem=send.at[sem],
+            recv_sem=recv.at[block],
+            device_id=(rep, where),
+            device_id_type=MESH,
+        )
+
+    def forward(act):
+        for d in range(Z):
+            for sign in (1, -1):
+                if d == 0 and sign < 0:
+                    continue
+                src = z - sign * d
+                ok = (src >= 0) & (src < Z)
+
+                def step(d=d, sign=sign, src=src):
+                    block = index_of(src, x, c)
+                    source = own if d == 0 else None
+                    if d > 0:
+                        act.wait(copy(block, 0, mine))
+                    if d == 0 or sign > 0:
+                        pl.when(z < Z - 1)(
+                            lambda: act(copy(block, d, index_of(z + 1, x, c), source))
+                        )
+                    if d == 0 or sign < 0:
+                        pl.when(z > 0)(
+                            lambda: act(copy(block, 4 + d, index_of(z - 1, x, c), source))
+                        )
+                    act(copy(block, 8 + src, index_of(z, 1 - x, c), source))
+                    act(copy(block, 12 + src, index_of(z, x, 1 - c), source))
+
+                if d == 0:
+                    step()
+                else:
+                    pl.when(ok)(step)
+        for d in range(Z):
+            for sign in (1, -1):
+                if d == 0 and sign < 0:
+                    continue
+                src = z - sign * d
+
+                def step(src=src):
+                    block = index_of(src, 1 - x, c)
+                    act.wait(copy(block, 0, mine))
+                    act(copy(block, 16 + src, index_of(z, x, 1 - c)))
+
+                pl.when((src >= 0) & (src < Z))(step)
+
+    class Start:
+        def __call__(self, op):
+            op.start()
+
+        def wait(self, op):
+            op.wait_recv()
+
+    class Finish:
+        def __call__(self, op):
+            op.wait_send()
+
+        def wait(self, op):
+            pass
+
+    forward(Start())
+    for a in range(Z):
+        for b in range(X):
+            copy(index_of(a, b, 1 - c), 0, mine).wait_recv()
+    forward(Finish())
+    local.wait()
+
+
+def expert_gather(value):
+    if (lax.axis_size("rep"), lax.axis_size("expert")) != (2, Z * X * C):
+        return lax.all_gather(value, "expert")
+    n = Z * X * C
+    return pl.pallas_call(
+        gather_kernel,
+        out_shape=jax.ShapeDtypeStruct((n,) + value.shape, value.dtype),
+        in_specs=[pl.BlockSpec(memory_space=pltpu.VMEM)],
+        out_specs=pl.BlockSpec(memory_space=pltpu.VMEM),
+        scratch_shapes=[
+            pltpu.SemaphoreType.DMA,
+            pltpu.SemaphoreType.DMA((20,)),
+            pltpu.SemaphoreType.DMA((n,)),
+        ],
+        compiler_params=pltpu.CompilerParams(
+            collective_id=0, has_side_effects=True, vmem_limit_bytes=24 << 20
+        ),
+    )(value)
+
+
+def reduce_kernel(value, out, acc, from_c, from_x, part, from_z, send, recv):
+    rep, z, x, c = place_of()
+    greet(rep, z, x, c)
+
+    def copy(source, target, sem, z2, x2, c2):
+        return pltpu.make_async_remote_copy(
+            src_ref=source,
+            dst_ref=target,
+            send_sem=send.at[sem],
+            recv_sem=recv.at[sem],
+            device_id=(rep, index_of(z2, x2, c2)),
+            device_id_type=MESH,
+        )
+
+    order = (Z - 1, 0, 1, 2)
+
+    def to_c(a, far):
+        b = 1 - x if far else x
+        k = (0 if far else Z) + a
+        return copy(value.at[index_of(a, b, 1 - c)], from_c.at[k], k, z, x, 1 - c)
+
+    def to_x(a):
+        return copy(acc.at[a], from_x.at[a], 8 + a, z, 1 - x, c)
+
+    def to_z(a, way):
+        k = way * Z + a
+        return copy(part.at[k], from_z.at[k], 12 + k, z + 1 - 2 * way, x, c)
+
+    def arrived(a, way):
+        k = way * Z + a
+        copy(part.at[k], from_z.at[k], 12 + k, z, x, 1 - c).wait_recv()
+
+    def wide(ref):
+        return ref.astype(F32)
+
+    for far in (True, False):
+        for a in order:
+            to_c(a, far).start()
+    for a in order:
+        to_c(a, True).wait_recv()
+        acc[a] = (wide(value[index_of(a, 1 - x, c)]) + wide(from_c[a])).astype(BF16)
+        to_x(a).start()
+    for a in order:
+        to_c(a, False).wait_recv()
+        acc[Z + a] = (wide(value[index_of(a, x, c)]) + wide(from_c[Z + a])).astype(BF16)
+    for a in order:
+        to_x(a).wait_recv()
+        acc[Z + a] = (wide(acc[Z + a]) + wide(from_x[a])).astype(BF16)
+
+        def first(way, a=a):
+            part[way * Z + a] = acc[Z + a]
+            to_z(a, way).start()
+
+        pl.when((z == 0) & (a > z))(functools.partial(first, 0))
+        pl.when((z == Z - 1) & (a < z))(functools.partial(first, 1))
+
+    def on(way, a):
+        k = way * Z + a
+        arrived(a, way)
+        part[k] = (wide(acc[Z + a]) + wide(from_z[k])).astype(BF16)
+        to_z(a, way).start()
+
+    for a in range(Z):
+        far = Z - 1 - a
+        pl.when((z > 0) & (far > z))(functools.partial(on, 0, far))
+        pl.when((z < Z - 1) & (a < z))(functools.partial(on, 1, a))
+    out[...] = wide(acc[Z + z])
+
+    def last(way):
+        arrived(z, way)
+        out[...] += wide(from_z[way * Z + z])
+
+    pl.when(z > 0)(functools.partial(last, 0))
+    pl.when(z < Z - 1)(functools.partial(last, 1))
+    for a in range(Z):
+        to_c(a, True).wait_send()
+        to_c(a, False).wait_send()
+        to_x(a).wait_send()
+        pl.when(a > z)(lambda a=a: to_z(a, 0).wait_send())
+        pl.when(a < z)(lambda a=a: to_z(a, 1).wait_send())
+
+
 def expert_reduce(value):
-    return lax.psum_scatter(value, "expert", scatter_dimension=0, tiled=False)
+    n, rows, width = value.shape
+    if (lax.axis_size("rep"), n) != (2, Z * X * C):
+        return lax.psum_scatter(value, "expert", scatter_dimension=0, tiled=False)
+    blocks = [pltpu.VMEM((k, rows, width), BF16) for k in (8, 8, 4, 8, 8)]
+    return pl.pallas_call(
+        reduce_kernel,
+        out_shape=jax.ShapeDtypeStruct((rows, width), F32),
+        in_specs=[pl.BlockSpec(memory_space=pltpu.VMEM)],
+        out_specs=pl.BlockSpec(memory_space=pltpu.VMEM),
+        scratch_shapes=blocks
+        + [pltpu.SemaphoreType.DMA((20,)), pltpu.SemaphoreType.DMA((20,))],
+        compiler_params=pltpu.CompilerParams(
+            collective_id=1, has_side_effects=True, vmem_limit_bytes=32 << 20
+        ),
+    )(value)
 
 
 def per_device(
@@ -67,7 +295,7 @@
         rest = rest - piece
     side = jnp.concatenate(pieces, axis=1)
     side = jnp.pad(side, ((0, 0), (0, -side.shape[1] % 128)))
-    both = lax.all_gather(jnp.concatenate([packed.astype(BF16), side], axis=1), "expert")
+    both = expert_gather(jnp.concatenate([packed.astype(BF16), side], axis=1))
     rows = both[:, :, :width]
     parts = both[:, :, width : width + 3 * aux.shape[1]].astype(F32)
     parts = parts.reshape(owners, packed_rows, 3, aux.shape[1])

time: 201 us -> 144 us (0.72)
  waiting for transfers between devices: 122 us -> 0.01 us
  Pallas kernels: 0 us -> 81.2 us
  between operations: 13.7 us -> 0.32 us
  other arithmetic: 10.4 us -> 7.78 us
  matrix products: 23.6 us -> 21.5 us
    pallas_call x0 -> x2, Pallas kernels: none -> 81.2 us  [the longest x1 47.7 us: expert_reduce(): pl.pallas_call(reduce_kernel, out_shape=jax.ShapeDtypeStruct((rows, width...]
    reduce_scatter x1 -> x0, waiting for transfers between devices: 57.8 us -> none  [expert_reduce(): return lax.psum_scatter(value, 'expert', scatter_dimension=0, tiled=False)]
    all_gather x1 -> x0, waiting for transfers between devices: 54.7 us -> none  [per_device(): lax.all_gather(jnp.concatenate([packed.astype(BF16), side], axis=1), 'exp...]
    ppermute x2, waiting for transfers between devices: 9.59 us -> 0.01 us  [rep_sum(): lax.ppermute(value.astype(BF16), 'rep', [(0, 1), (1, 0)]).astype(F32)]
    unnamed x10 -> x12, local copies, waits for them, and re-layouts: 0.03 us -> 2.05 us
  transfers between devices with their start and end apart: 4 -> 2, of which waited for: 4 -> 0; matrix products, arithmetic and copies ran while one was open for 13% -> 21% of each run, Pallas kernels for 0% -> 0%
where the time goes in v1:
time: 144 us
  Pallas kernels  81.2 us (56%)
  local copies, waits for them, and re-layouts  25.7 us (18%)
  matrix products  21.5 us (15%)
  other arithmetic  7.78 us (5%)
  blocking collectives  5.01 us (3%)
  starting transfers between devices  2.03 us (1%)
    pallas_call x1, Pallas kernels, expert_reduce(): pl.pallas_call(reduce_kernel, out_shape=jax.ShapeDtypeStruct((rows, width...  47.7 us
    pallas_call x1, Pallas kernels, expert_gather(): pl.pallas_call(gather_kernel, out_shape=jax.ShapeDtypeStruct((n,) + value...  33.6 us
    dot_general x2, matrix products, per_device(): out = jnp.dot(act, down_weight[e], preferred_element_type=F32).astype(BF16)  7.58 us
    reshape x1, local copies, waits for them, and re-layouts, per_device(): rows.reshape(owners, owners, hand_cap, width)  7.21 us
    dot_general x2, matrix products, per_device(): jnp.dot(flat, up_weight[e], preferred_element_type=F32)  6.98 us
    select_n x1, local copies, waits for them, and re-layouts, per_device(): jnp.where(same[None, :, None, :, None], gate_slot[:, :, :, None, :], 0)  5.93 us
    psum x1, blocking collectives, per_device(): lax.psum(aux[:, :, experts_all], 'rep') / (width * reps) + 1e-06  5.01 us
    slice x1, local copies, waits for them, and re-layouts, per_device(): rows = both[:, :, :width]  4.74 us
  transfers between devices with their start and end apart: 2, of which 0 were waited for; matrix products, arithmetic and copies ran while one was open for 21% of the time, Pallas kernels for 0%

profile of v1, /device:TPU:0, one launch (start us, length us, event | category | flops | bytes accessed | tf_op | source)
XLA Modules:
  0.0 143.6 jit_solution(16615730648740446915)
XLA Ops:
  0.0 0.7 broadcast_compare_fusion.1
  0.7 0.9 fusion.19
  1.6 0.7 add_select_fusion
  2.3 0.3 fusion.46
  2.7 0.7 select_reduce_fusion.2
  3.5 0.3 select_reduce_fusion.1
  4.0 33.6 %shard_map.82 = bf16[16,64,2176]{2,1,0:T(8,128)(2,1)S(1)} custom-call(bf16[64,2176]{1,0:T(8,128)(2,1)S(1)} %pad_maximum_fusion.1.own), custom_call_target="tpu_custom_call" | custom-call | tf_op jit(solution)/shard_map/pallas_call | solution.py:137
  37.6 2.0 %copy-done.1 = bf16[16,64,2176]{2,1,0:T(8,128)(2,1)} copy-done((bf16[16,64,2176]{2,1,0:T(8,128)(2,1)}, bf16[16,64,2176]{2,1,0:T(8,128)(2,1)S(1)}, u32[]{:S(2)}) %copy-start.1) | copy-done | bytes 4456472
  39.7 0.4 copy.53
  40.3 5.0 %psum.7 = f32[16,64]{1,0:T(8,128)S(1)} all-reduce(f32[16,64]{1,0:T(8,128)S(1)} %slice_bitcast_fusion), channel_id=1, replica_groups=mesh['rep'=2,'expert'=16] {'rep'}, use_global_device_ids=true, to_apply=%region_4.5 | all-reduce | flops 1024 | bytes 8192 | tf_op jit(solution)/shard_map/psum | solution.py:303
  45.8 0.3 select_reduce_fusion
  46.3 0.8 copy.61
  47.2 0.7 copy.60
  47.9 3.3 %multiply_convert_fusion = bf16[16,32,2048]{2,1,0:T(8,128)(2,1)S(1)} fusion(f32[2048]{0:T(1024)S(1)} %copy-done.2, f32[16,32]{1,0:T(8,128)S(1)} %copy.63, pred[16,64,32]{1,2,0:T(32,128)(4,1)S(1)} %copy.61, s32[16,64,32]{1,2,0:T(8,128)S(1)} %copy.60, s32[32]{0:T(128)S(1)} %eq.119, bf16[16,64,2176]{2,1,0:T(8,128)(2,1)} %copy-done.1), kind=kOutput, calls=%fused_computation.12 | convolution fusion | flops 137428992 | bytes 6465664 | tf_op jit(solution)/shard_map/irs,ird->isd/dot_general | solution.py:313
  51.4 4.6 %fusion.48 = (bf16[256,1024]{1,0:T(8,128)(2,1)S(1)}, f32[256,1024]{1,0:T(8,128)}) fusion(bf16[256,2048]{1,0:T(8,128)(2,1)S(1)} %bitcast.77, bf16[2,2048,1024]{2,1,0:T(8,128)(2,1)} %param.14), kind=kOutput, calls=%fused_computation.80 | convolution fusion | flops 1074003968 | bytes 6815744 | tf_op jit(solution)/shard_map/dot_general | solution.py:323
  56.0 1.5 %collective-permute-start = (bf16[256,1024]{1,0:T(8,128)(2,1)S(1)}, bf16[256,1024]{1,0:T(8,128)(2,1)S(1)}, u32[]{:S(2)}, u32[]{:S(2)}) collective-permute-start(bf16[256,1024]{1,0:T(8,128)(2,1)S(1)} %get-tuple-element.17), channel_id=1, source_target_pairs={{0,16},{16,0},{1,17},{17,1},{2,18},{18,2},{3,19},{19,3},{4,20},{20... | collective-permute-start | bytes 1572872 | tf_op jit(solution)/shard_map/ppermute | solution.py:22
  57.5 2.4 %fusion.47 = (bf16[256,1024]{1,0:T(8,128)(2,1)}, f32[256,1024]{1,0:T(8,128)}) fusion(bf16[256,2048]{1,0:T(8,128)(2,1)S(1)} %bitcast.75, bf16[2,2048,1024]{2,1,0:T(8,128)(2,1)S(1)} %bitcast.82), kind=kOutput, calls=%fused_computation.79 | convolution fusion | flops 1074003968 | bytes 6815744 | tf_op jit(solution)/shard_map/dot_general | solution.py:323
  59.9 0.5 collective-permute-start.1
  60.4 4.7 %slice.36 = bf16[16,64,2048]{2,1,0:T(8,128)(2,1)} slice(bf16[16,64,2176]{2,1,0:T(8,128)(2,1)} %copy-done.1), slice={[0:16], [0:64], [0:2048]} | slice | bytes 8388608 | tf_op jit(solution)/shard_map/slice | solution.py:299
  65.2 0.4 copy.57
  65.6 0.3 copy.58
  65.8 1.4 broadcast_in_dim.110
  67.5 0.3 copy.66
  67.9 7.2 %reshape.92 = bf16[16,16,4,2048]{3,2,1,0:T(4,128)(2,1)} reshape(bf16[16,64,2048]{2,1,0:T(8,128)(2,1)} %slice.36) | data formatting | bytes 8388608 | tf_op jit(solution)/shard_map/reshape | solution.py:340
  75.2 1.0 bitcast_convert_fusion
  76.6 2.4 %broadcast_select_fusion = bf16[16,16,4,16,32]{4,3,2,1,0:T(8,128)(2,1)} fusion(pred[16,16]{1,0:T(8,128)(4,1)S(1)} %iota_compare_fusion.7, bf16[16,16,4,32]{3,2,1,0:T(4,128)(2,1)S(1)} %copy.59), kind=kLoop, calls=%fused_computation.13 | loop fusion | flops 524288 | bytes 1114368 | tf_op jit(solution)/shard_map/jit(_where)/select_n | solution.py:335
  78.9 5.9 %select_n.49 = bf16[1024,512]{1,0:T(8,128)(2,1)S(1)} reshape(bf16[16,16,4,16,32]{4,3,2,1,0:T(8,128)(2,1)} %broadcast_select_fusion) | data formatting | bytes 2097152 | tf_op jit(solution)/shard_map/jit(_where)/select_n | solution.py:335
  84.9 3.9 %fusion.12 = bf16[256,2048]{1,0:T(8,128)(2,1)S(1)} fusion(bf16[2,1024,2048]{2,1,0:T(8,128)(2,1)} %param.15, f32[256,1024]{1,0:T(8,128)} %get-tuple-element.18, bf16[256,1024]{1,0:T(8,128)(2,1)S(1)} %collective-permute-done), kind=kOutput, calls=%fused_computation.15 | convolution fusion | flops 1076101120 | bytes 6815744 | tf_op jit(solution)/shard_map/dot_general | solution.py:327
  88.8 3.7 %fusion.15 = bf16[256,2048]{1,0:T(8,128)(2,1)S(1)} fusion(bf16[2,1024,2048]{2,1,0:T(8,128)(2,1)} %param.15, f32[256,1024]{1,0:T(8,128)S(1)} %copy-done.3, bf16[256,1024]{1,0:T(8,128)(2,1)} %collective-permute-done.1), kind=kOutput, calls=%fused_computation.16 | convolution fusion | flops 1076101120 | bytes 6815744 | tf_op jit(solution)/shard_map/dot_general | solution.py:327
  92.7 2.3 %convolution_convert_fusion = bf16[1024,2048]{1,0:T(8,128)(2,1)S(1)} fusion(bf16[1024,512]{1,0:T(8,128)(2,1)S(1)} %select_n.49, bf16[512,2048]{1,0:T(8,128)(2,1)S(1)} %bitcast.74), kind=kOutput, calls=%fused_computation.14 | convolution fusion | flops 2149580800 | bytes 7340032 | tf_op jit(solution)/shard_map/dot_general | solution.py:337
  95.1 47.7 %shard_map.83 = f32[64,2048]{1,0:T(8,128)S(1)} custom-call(bf16[16,64,2048]{2,1,0:T(8,128)(2,1)S(1)} %bitcast.66), custom_call_target="tpu_custom_call" | custom-call | tf_op jit(solution)/shard_map/pallas_call | solution.py:240
  142.7 0.9 add.57
  (41 shorter events, 2.3 us)
Async XLA Ops:
  0.0 2.3 %copy-start = (bf16[128,2048]{1,0:T(8,128)(2,1)S(1)}, bf16[128,2048]{1,0:T(8,128)(2,1)}, u32[]{:S(2)}) copy-start(bf16[128,2048]{1,0:T(8,128)(2,1)} %param.8) | copy-start | bytes 1572868
  37.6 2.0 %copy-start.1 = (bf16[16,64,2176]{2,1,0:T(8,128)(2,1)}, bf16[16,64,2176]{2,1,0:T(8,128)(2,1)S(1)}, u32[]{:S(2)}) copy-start(bf16[16,64,2176]{2,1,0:T(8,128)(2,1)S(1)} %shard_map.82) | copy-start | bytes 13369348
  39.6 8.3 %copy-start.2 = (f32[2048]{0:T(1024)S(1)}, f32[2048]{0:T(1024)}, u32[]{:S(2)}) copy-start(f32[2048]{0:T(1024)} %param.9) | copy-start | bytes 24580
  47.9 9.6 %slice-start = ((s8[8388608]{0:T(1024)(128)(4,1)}), s8[4194304]{0:T(1024)(128)(4,1)S(1)}, s32[]{:S(2)}) async-start(s8[8388608]{0:T(1024)(128)(4,1)} %bitcast.81), calls=%async_computation | async-start | bytes 8388608
  51.2 6.3 %slice-start.1 = ((s8[8388608]{0:T(1024)(128)(4,1)}), s8[4194304]{0:T(1024)(128)(4,1)S(1)}, s32[]{:S(2)}) async-start(s8[8388608]{0:T(1024)(128)(4,1)} %bitcast.81), calls=%async_computation.1 | async-start | bytes 8388608
  56.0 28.9 %collective-permute-start = (bf16[256,1024]{1,0:T(8,128)(2,1)S(1)}, bf16[256,1024]{1,0:T(8,128)(2,1)S(1)}, u32[]{:S(2)}, u32[]{:S(2)}) collective-permute-start(bf16[256,1024]{1,0:T(8,128)(2,1)S(1)} %get-tuple-element.17), channel_id=1, source_target_pairs={{0,16},{16,0},{1,17},{17,1},{2,18},{18,2},{3,19},{19,3},{4,20},{20... | collective-permute-start | bytes 1572872 | tf_op jit(solution)/shard_map/ppermute | solution.py:22
  59.9 28.9 %collective-permute-start.1 = (bf16[256,1024]{1,0:T(8,128)(2,1)}, bf16[256,1024]{1,0:T(8,128)(2,1)}, u32[]{:S(2)}, u32[]{:S(2)}) collective-permute-start(bf16[256,1024]{1,0:T(8,128)(2,1)} %get-tuple-element.15), channel_id=1, source_target_pairs={{0,16},{16,0},{1,17},{17,1},{2,18},{18,2},{3,19},{19,3},{4,20},{20... | collective-permute-start | bytes 1572872 | tf_op jit(solution)/shard_map/ppermute | solution.py:22
  84.9 3.9 %copy-start.3 = (f32[256,1024]{1,0:T(8,128)S(1)}, f32[256,1024]{1,0:T(8,128)}, u32[]{:S(2)}) copy-start(f32[256,1024]{1,0:T(8,128)} %get-tuple-element.16) | copy-start | bytes 3145732

commit v2 on v1

--- a/solution.py
+++ b/solution.py
@@ -16,10 +16,10 @@
     return (i[:, None] > i[None, :]).astype(BF16)
 
 
-def rep_sum(value, reps):
+def rep_sum(value, reps, kind=BF16):
     if reps != 2:
         return lax.psum(value, "rep")
-    return value + lax.ppermute(value.astype(BF16), "rep", [(0, 1), (1, 0)]).astype(F32)
+    return value + lax.ppermute(value.astype(kind), "rep", [(0, 1), (1, 0)]).astype(F32)
 
 
 Z, X, C = 4, 2, 2
@@ -195,27 +195,25 @@
     for a in order:
         to_c(a, False).wait_recv()
         acc[Z + a] = (wide(value[index_of(a, x, c)]) + wide(from_c[Z + a])).astype(BF16)
-    for a in order:
-        to_x(a).wait_recv()
-        acc[Z + a] = (wide(acc[Z + a]) + wide(from_x[a])).astype(BF16)
-
-        def first(way, a=a):
-            part[way * Z + a] = acc[Z + a]
-            to_z(a, way).start()
-
-        pl.when((z == 0) & (a > z))(functools.partial(first, 0))
-        pl.when((z == Z - 1) & (a < z))(functools.partial(first, 1))
-
     def on(way, a):
         k = way * Z + a
         arrived(a, way)
         part[k] = (wide(acc[Z + a]) + wide(from_z[k])).astype(BF16)
         to_z(a, way).start()
 
-    for a in range(Z):
-        far = Z - 1 - a
-        pl.when((z > 0) & (far > z))(functools.partial(on, 0, far))
+    for a in order:
+        to_x(a).wait_recv()
+        acc[Z + a] = (wide(acc[Z + a]) + wide(from_x[a])).astype(BF16)
+
+        def first(way, a=a):
+            part[way * Z + a] = acc[Z + a]
+            to_z(a, way).start()
+
+        pl.when((z == 0) & (a > z))(functools.partial(first, 0))
+        pl.when((z == Z - 1) & (a < z))(functools.partial(first, 1))
+        pl.when((z > 0) & (a > z))(functools.partial(on, 0, a))
         pl.when((z < Z - 1) & (a < z))(functools.partial(on, 1, a))
+
     out[...] = wide(acc[Z + z])
 
     def last(way):
@@ -296,11 +294,10 @@
     side = jnp.concatenate(pieces, axis=1)
     side = jnp.pad(side, ((0, 0), (0, -side.shape[1] % 128)))
     both = expert_gather(jnp.concatenate([packed.astype(BF16), side], axis=1))
-    rows = both[:, :, :width]
     parts = both[:, :, width : width + 3 * aux.shape[1]].astype(F32)
     parts = parts.reshape(owners, packed_rows, 3, aux.shape[1])
     aux = parts[:, :, 0] + parts[:, :, 1] + parts[:, :, 2]
-    rinv = lax.rsqrt(lax.psum(aux[:, :, experts_all], "rep") / (width * reps) + 1e-06)
+    rinv = lax.rsqrt(rep_sum(aux[:, :, experts_all], reps, F32) / (width * reps) + 1e-06)
 
     me = lax.axis_index("expert")
     gates = lax.dynamic_slice_in_dim(aux, me * local_experts, local_experts, axis=2)
@@ -310,7 +307,9 @@
     ).astype(jnp.int32)
     hot = (place[:, :, :, None] == jnp.arange(cap)) & (routed > 0)[:, :, :, None]
     hot = hot.reshape(owners, packed_rows, local_experts * cap)
-    slots = jnp.einsum("irs,ird->isd", hot.astype(BF16), rows, preferred_element_type=F32)
+    slots = jnp.einsum("irs,ird->isd", hot.astype(BF16), both, preferred_element_type=F32)[
+        :, :, :width
+    ]
     rinv_slot = jnp.sum(jnp.where(hot, rinv[:, :, None], 0.0), axis=1)
     normed = (slots * rinv_slot[:, :, None] * norm_gain).astype(BF16)
     normed = normed.reshape(owners, local_experts, cap, width)
@@ -331,14 +330,16 @@
 
     gate_slot = jnp.where(hot, jnp.repeat(gates, cap, axis=2), 0.0).astype(BF16)
     gate_slot = gate_slot.reshape(owners, owners, hand_cap, -1).transpose(1, 0, 2, 3)
-    same = jnp.arange(owners)[:, None] == jnp.arange(owners)[None, :]
-    weights = jnp.where(same[None, :, None, :, None], gate_slot[:, :, :, None, :], 0)
-    weights = weights.reshape(owners * packed_rows, -1)
+    count = local_experts * cap
+    gate_slot = gate_slot.reshape(owners * packed_rows, count)
+    column = jnp.arange(owners * count)
+    spread = (jnp.arange(count)[:, None] == column[None, :] % count).astype(BF16)
+    block = jnp.arange(owners * packed_rows) // hand_cap % owners
+    weights = jnp.dot(gate_slot, spread, preferred_element_type=F32)
+    weights = jnp.where(block[:, None] == column[None, :] // count, weights, 0.0).astype(BF16)
     mix = jnp.dot(weights, out, preferred_element_type=F32).astype(BF16)
     summed = expert_reduce(mix.reshape(owners, packed_rows, width))
-    own = lax.dynamic_slice_in_dim(
-        rows.reshape(owners, owners, hand_cap, width), me, 1, axis=1
-    )[:, 0]
+    own = lax.dynamic_slice_in_dim(both, me * hand_cap, hand_cap, axis=1)[:, :, :width]
     return own.reshape(packed_rows, width).astype(F32) + summed.astype(F32)
 
 

time: 144 us -> 135 us (0.938)
  waiting for transfers between devices: 0.01 us -> 20.4 us
  local copies, waits for them, and re-layouts: 25.7 us -> 12.6 us
  Pallas kernels: 81.2 us -> 73.1 us
  matrix products: 21.5 us -> 16.3 us
  blocking collectives: 5.01 us -> 0 us
  starting transfers between devices: 2.03 us -> 3.71 us
    ppermute x2 -> x3, waiting for transfers between devices: 0.01 us -> 20.4 us  [rep_sum(): lax.ppermute(value.astype(kind), 'rep', [(0, 1), (1, 0)]).astype(F32)]
    pallas_call x1, Pallas kernels: 47.7 us -> 39.5 us  [expert_reduce(): pl.pallas_call(reduce_kernel, out_shape=jax.ShapeDtypeStruct((rows, width...]
    reshape x1 -> x0, local copies, waits for them, and re-layouts: 7.21 us -> none  [per_device(): rows.reshape(owners, owners, hand_cap, width)]
    select_n x1 -> x0, local copies, waits for them, and re-layouts: 5.93 us -> none  [per_device(): jnp.where(same[None, :, None, :, None], gate_slot[:, :, :, None, :], 0)]
    psum x1 -> x0, blocking collectives: 5.01 us -> none  [per_device(): lax.psum(aux[:, :, experts_all], 'rep') / (width * reps) + 1e-06]
    dot_general x2, matrix products: 7.58 us -> 2.65 us  [per_device(): out = jnp.dot(act, down_weight[e], preferred_element_type=F32).astype(BF16)]
    slice x1 -> x0, local copies, waits for them, and re-layouts: 4.74 us -> none  [per_device(): rows = both[:, :, :width]]
    unnamed x12 -> x18, local copies, waits for them, and re-layouts: 2.05 us -> 4.98 us
  transfers between devices with their start and end apart: 2 -> 3, of which waited for: 0 -> 2; matrix products, arithmetic and copies ran while one was open for 21% -> 8% of each run, Pallas kernels for 0% -> 0%
where the time goes in v2:
time: 135 us; the launch traced here: 134 us
  Pallas kernels  73.1 us (54%)
  waiting for transfers between devices  20.4 us (15%)
  matrix products  16.3 us (12%)
  local copies, waits for them, and re-layouts  12.6 us (9%)
  other arithmetic  7.89 us (6%)
  starting transfers between devices  3.71 us (3%)
    pallas_call x1, Pallas kernels, expert_reduce(): pl.pallas_call(reduce_kernel, out_shape=jax.ShapeDtypeStruct((rows, width...  39.5 us
    pallas_call x1, Pallas kernels, expert_gather(): pl.pallas_call(gather_kernel, out_shape=jax.ShapeDtypeStruct((n,) + value...  33.6 us
    ppermute x3, waiting for transfers between devices, rep_sum(): lax.ppermute(value.astype(kind), 'rep', [(0, 1), (1, 0)]).astype(F32)  20.4 us
    unnamed x18, local copies, waits for them, and re-layouts  4.98 us
    dot_general x2, matrix products, per_device(): jnp.dot(flat, up_weight[e], preferred_element_type=F32)  4.87 us
    dot_general x1, matrix products, per_device(): mix = jnp.dot(weights, out, preferred_element_type=F32).astype(BF16)  4.13 us
    ppermute x3, starting transfers between devices, rep_sum(): lax.ppermute(value.astype(kind), 'rep', [(0, 1), (1, 0)]).astype(F32)  3.71 us
    dot_general x1, matrix products, per_device(): jnp.einsum('irs,ird->isd', hot.astype(BF16), both, preferred_element_type...  3.3 us
  transfers between devices with their start and end apart: 3, of which 2 were waited for; matrix products, arithmetic and copies ran while one was open for 8% of the time, Pallas kernels for 0%

profile of v2, /device:TPU:0, one launch (start us, length us, event | category | flops | bytes accessed | tf_op | source)
XLA Modules:
  0.0 134.3 jit_solution(8598621363107152311)
XLA Ops:
  0.0 0.7 broadcast_compare_fusion.1
  0.7 0.9 fusion.23
  1.6 0.7 add_select_fusion.3
  2.7 0.7 select_reduce_fusion.2
  4.0 33.6 %shard_map.82 = bf16[16,64,2176]{2,1,0:T(8,128)(2,1)S(1)} custom-call(bf16[64,2176]{1,0:T(8,128)(2,1)S(1)} %pad_maximum_fusion.1.own), custom_call_target="tpu_custom_call" | custom-call | tf_op jit(solution)/shard_map/pallas_call | solution.py:137
  37.6 2.0 %copy-done.1 = bf16[16,64,2176]{2,1,0:T(8,128)(2,1)} copy-done((bf16[16,64,2176]{2,1,0:T(8,128)(2,1)}, bf16[16,64,2176]{2,1,0:T(8,128)(2,1)S(1)}, u32[]{:S(2)}) %copy-start.1) | copy-done | bytes 4456472
  39.7 0.4 copy.48
  40.1 0.8 fusion.75
  40.9 0.7 slice_bitcast_fusion
  41.6 1.6 %collective-permute-start = (f32[16,64]{1,0:T(8,128)S(1)}, f32[16,64]{1,0:T(8,128)S(1)}, u32[]{:S(2)}, u32[]{:S(2)}) collective-permute-start(f32[16,64]{1,0:T(8,128)S(1)} %slice_bitcast_fusion), channel_id=1, source_target_pairs={{0,16},{16,0},{1,17},{17,1},{2,18},{18,2},{3,19},{19,3},{4,20},{20... | collective-permute-start | bytes 12296 | tf_op jit(solution)/shard_map/ppermute | solution.py:22
  43.2 1.2 dynamic-slice_convert_fusion
  45.1 1.2 broadcast_in_dim.93
  46.7 1.0 copy.52
  48.2 1.1 fusion.30
  49.4 0.8 copy.56
  50.3 0.7 copy.55
  50.9 0.8 copy.54
  51.8 0.7 add_rsqrt_fusion
  53.0 3.3 %multiply_convert_fusion = bf16[16,32,2048]{2,1,0:T(8,128)(2,1)S(1)} fusion(bf16[16,64,2176]{2,1,0:T(8,128)(2,1)} %copy-done.1, f32[2048]{0:T(1024)S(1)} %copy-done.4, f32[16,32]{1,0:T(8,128)S(1)} %copy.58, pred[16,64,32]{1,2,0:T(32,128)(4,1)S(1)} %copy.56, s32[16,64,32]{1,2,0:T(8,128)S(1)} %copy.55, s32[32]{0:T(128)S(1)} %eq.132), kind=kOutput, calls=%fused_computation.14 | convolution fusion | flops 137428992 | bytes 6465664 | tf_op jit(solution)/shard_map/irs,ird->isd/dot_general | solution.py:310
  56.5 3.6 %fusion.67 = (bf16[256,1024]{1,0:T(8,128)(2,1)S(1)}, f32[256,1024]{1,0:T(8,128)S(1)}) fusion(bf16[256,2048]{1,0:T(8,128)(2,1)S(1)} %bitcast.74, bf16[2,2048,1024]{2,1,0:T(8,128)(2,1)} %param.14), kind=kOutput, calls=%fused_computation.107 | convolution fusion | flops 1074003968 | bytes 6815744 | tf_op jit(solution)/shard_map/dot_general | solution.py:322
  60.1 0.6 collective-permute-start.2
  60.7 1.3 fusion.68
  61.9 1.6 %collective-permute-start.1 = (bf16[256,1024]{1,0:T(8,128)(2,1)S(1)}, bf16[256,1024]{1,0:T(8,128)(2,1)S(1)}, u32[]{:S(2)}, u32[]{:S(2)}) collective-permute-start(bf16[256,1024]{1,0:T(8,128)(2,1)S(1)} %get-tuple-element.17), channel_id=1, source_target_pairs={{0,16},{16,0},{1,17},{17,1},{2,18},{18,2},{3,19},{19,3},{4,20},{20... | collective-permute-start | bytes 1572872 | tf_op jit(solution)/shard_map/ppermute | solution.py:22
  63.5 11.4 %collective-permute-done.2 = bf16[256,1024]{1,0:T(8,128)(2,1)S(1)} collective-permute-done((bf16[256,1024]{1,0:T(8,128)(2,1)S(1)}, bf16[256,1024]{1,0:T(8,128)(2,1)S(1)}, u32[]{:S(2)}, u32[]{:S(2)}) %collective-permute-start.2) | collective-permute-done | bytes 524320 | tf_op jit(solution)/shard_map/ppermute | solution.py:22
  74.9 1.3 fusion.19
  76.3 9.0 %collective-permute-done.1 = bf16[256,1024]{1,0:T(8,128)(2,1)S(1)} collective-permute-done((bf16[256,1024]{1,0:T(8,128)(2,1)S(1)}, bf16[256,1024]{1,0:T(8,128)(2,1)S(1)}, u32[]{:S(2)}, u32[]{:S(2)}) %collective-permute-start.1) | collective-permute-done | bytes 524320 | tf_op jit(solution)/shard_map/ppermute | solution.py:22
  85.3 1.3 fusion.16
  86.8 0.7 copy-done.3
  87.6 4.1 %convolution_convert_fusion = bf16[1024,2048]{1,0:T(8,128)(2,1)} fusion(bf16[512,2048]{1,0:T(8,128)(2,1)S(1)} %bitcast.71, bf16[1024,32]{1,0:T(8,128)(2,1)S(1)} %bitcast.76, s32[512]{0:T(512)S(1)} %get-tuple-element.20, s32[1024]{0:T(1024)S(1)} %add_select_fusion, s32[512]{0:T(512)S(1)} %get-tuple-element.19), kind=kOutput, calls=%fused_computation.15 | convolution fusion | flops 2184724480 | bytes 6365184 | tf_op jit(solution)/shard_map/dot_general | solution.py:340
  91.7 2.2 %copy-done.2 = bf16[1024,2048]{1,0:T(8,128)(2,1)S(1)} copy-done((bf16[1024,2048]{1,0:T(8,128)(2,1)S(1)}, bf16[1024,2048]{1,0:T(8,128)(2,1)}, u32[]{:S(2)}) %copy-start.2) | copy-done | bytes 4194328
  93.9 39.5 %shard_map.83 = f32[64,2048]{1,0:T(8,128)S(1)} custom-call(bf16[16,64,2048]{2,1,0:T(8,128)(2,1)S(1)} %bitcast.63), custom_call_target="tpu_custom_call" | custom-call | tf_op jit(solution)/shard_map/pallas_call | solution.py:238
  133.4 0.9 add.93
  (46 shorter events, 3.6 us)
Async XLA Ops:
  0.0 2.3 %copy-start = (bf16[128,2048]{1,0:T(8,128)(2,1)S(1)}, bf16[128,2048]{1,0:T(8,128)(2,1)}, u32[]{:S(2)}) copy-start(bf16[128,2048]{1,0:T(8,128)(2,1)} %param.8) | copy-start | bytes 1572868
  37.6 2.0 %copy-start.1 = (bf16[16,64,2176]{2,1,0:T(8,128)(2,1)}, bf16[16,64,2176]{2,1,0:T(8,128)(2,1)S(1)}, u32[]{:S(2)}) copy-start(bf16[16,64,2176]{2,1,0:T(8,128)(2,1)S(1)} %shard_map.82) | copy-start | bytes 13369348
  41.6 10.2 %collective-permute-start = (f32[16,64]{1,0:T(8,128)S(1)}, f32[16,64]{1,0:T(8,128)S(1)}, u32[]{:S(2)}, u32[]{:S(2)}) collective-permute-start(f32[16,64]{1,0:T(8,128)S(1)} %slice_bitcast_fusion), channel_id=1, source_target_pairs={{0,16},{16,0},{1,17},{17,1},{2,18},{18,2},{3,19},{19,3},{4,20},{20... | collective-permute-start | bytes 12296 | tf_op jit(solution)/shard_map/ppermute | solution.py:22
  46.6 6.3 %copy-start.4 = (f32[2048]{0:T(1024)S(1)}, f32[2048]{0:T(1024)}, u32[]{:S(2)}) copy-start(f32[2048]{0:T(1024)} %param.9) | copy-start | bytes 24580
  53.0 7.7 %slice-start = ((s8[8388608]{0:T(1024)(128)(4,1)}), s8[4194304]{0:T(1024)(128)(4,1)S(1)}, s32[]{:S(2)}) async-start(s8[8388608]{0:T(1024)(128)(4,1)} %bitcast.79), calls=%async_computation | async-start | bytes 8388608
  56.3 4.4 %slice-start.1 = ((s8[8388608]{0:T(1024)(128)(4,1)}), s8[4194304]{0:T(1024)(128)(4,1)S(1)}, s32[]{:S(2)}) async-start(s8[8388608]{0:T(1024)(128)(4,1)} %bitcast.79), calls=%async_computation.1 | async-start | bytes 8388608
  56.4 18.5 %slice-start.2 = ((s8[8388608]{0:T(1024)(128)(4,1)}), s8[4194304]{0:T(1024)(128)(4,1)S(1)}, s32[]{:S(2)}) async-start(s8[8388608]{0:T(1024)(128)(4,1)} %bitcast.81), calls=%async_computation.2 | async-start | bytes 8388608
  60.1 14.8 %collective-permute-start.2 = (bf16[256,1024]{1,0:T(8,128)(2,1)S(1)}, bf16[256,1024]{1,0:T(8,128)(2,1)S(1)}, u32[]{:S(2)}, u32[]{:S(2)}) collective-permute-start(bf16[256,1024]{1,0:T(8,128)(2,1)S(1)} %get-tuple-element.15), channel_id=1, source_target_pairs={{0,16},{16,0},{1,17},{17,1},{2,18},{18,2},{3,19},{19,3},{4,20},{20... | collective-permute-start | bytes 1572872 | tf_op jit(solution)/shard_map/ppermute | solution.py:22
  60.7 14.3 %slice-start.3 = ((s8[8388608]{0:T(1024)(128)(4,1)}), s8[4194304]{0:T(1024)(128)(4,1)S(1)}, s32[]{:S(2)}) async-start(s8[8388608]{0:T(1024)(128)(4,1)} %bitcast.81), calls=%async_computation.3 | async-start | bytes 8388608
  61.9 23.3 %collective-permute-start.1 = (bf16[256,1024]{1,0:T(8,128)(2,1)S(1)}, bf16[256,1024]{1,0:T(8,128)(2,1)S(1)}, u32[]{:S(2)}, u32[]{:S(2)}) collective-permute-start(bf16[256,1024]{1,0:T(8,128)(2,1)S(1)} %get-tuple-element.17), channel_id=1, source_target_pairs={{0,16},{16,0},{1,17},{17,1},{2,18},{18,2},{3,19},{19,3},{4,20},{20... | collective-permute-start | bytes 1572872 | tf_op jit(solution)/shard_map/ppermute | solution.py:22
  86.6 1.0 copy-start.3
  91.7 2.2 %copy-start.2 = (bf16[1024,2048]{1,0:T(8,128)(2,1)S(1)}, bf16[1024,2048]{1,0:T(8,128)(2,1)}, u32[]{:S(2)}) copy-start(bf16[1024,2048]{1,0:T(8,128)(2,1)} %convolution_convert_fusion) | copy-start | bytes 12582916

commit v3 on v2

--- a/solution.py
+++ b/solution.py
@@ -318,9 +318,11 @@
     sums = []
     for e in range(local_experts):
         flat = normed[:, e].reshape(owners * cap, width)
-        sums.append(
-            rep_sum(jnp.dot(flat, up_weight[e], preferred_element_type=F32), reps)
-        )
+        halves = [
+            rep_sum(jnp.dot(flat, part, preferred_element_type=F32), reps)
+            for part in jnp.split(up_weight[e], 2, axis=1)
+        ]
+        sums.append(jnp.concatenate(halves, axis=1))
     for e in range(local_experts):
         act = jax.nn.silu(sums[e]).astype(BF16)
         out = jnp.dot(act, down_weight[e], preferred_element_type=F32).astype(BF16)

time: 135 us -> 138 us (1.022)
  local copies, waits for them, and re-layouts: 12.6 us -> 18.6 us
  waiting for transfers between devices: 20.4 us -> 17.9 us
  matrix products: 16.3 us -> 14.3 us
  starting transfers between devices: 3.71 us -> 5.71 us
    squeeze x0 -> x1, local copies, waits for them, and re-layouts: none -> 6 us  [per_device(): up_weight[e]]
    ppermute x3 -> x5, waiting for transfers between devices: 20.4 us -> 17.9 us  [rep_sum(): lax.ppermute(value.astype(kind), 'rep', [(0, 1), (1, 0)]).astype(F32)]
    ppermute x3 -> x5, starting transfers between devices: 3.71 us -> 5.71 us  [rep_sum(): lax.ppermute(value.astype(kind), 'rep', [(0, 1), (1, 0)]).astype(F32)]
    dot_general x2 -> x4, matrix products: 4.87 us -> 2.96 us  [per_device(): jnp.dot(flat, part, preferred_element_type=F32)]
    unnamed x18 -> x20, local copies, waits for them, and re-layouts: 4.98 us -> 4.99 us
  transfers between devices with their start and end apart: 3 -> 5, of which waited for: 2 -> 4; matrix products, arithmetic and copies ran while one was open for 8% -> 12% of each run, Pallas kernels for 0% -> 0%
where the time goes in v3:
time: 138 us; the launch traced here: 137 us
  Pallas kernels  73.1 us (53%)
  local copies, waits for them, and re-layouts  18.6 us (13%)
  waiting for transfers between devices  17.9 us (13%)
  matrix products  14.3 us (10%)
  other arithmetic  7.27 us (5%)
  starting transfers between devices  5.71 us (4%)
    pallas_call x1, Pallas kernels, expert_reduce(): pl.pallas_call(reduce_kernel, out_shape=jax.ShapeDtypeStruct((rows, width...  39.5 us
    pallas_call x1, Pallas kernels, expert_gather(): pl.pallas_call(gather_kernel, out_shape=jax.ShapeDtypeStruct((n,) + value...  33.6 us
    ppermute x5, waiting for transfers between devices, rep_sum(): lax.ppermute(value.astype(kind), 'rep', [(0, 1), (1, 0)]).astype(F32)  17.9 us
    squeeze x1, local copies, waits for them, and re-layouts, per_device(): up_weight[e]  6 us
    ppermute x5, starting transfers between devices, rep_sum(): lax.ppermute(value.astype(kind), 'rep', [(0, 1), (1, 0)]).astype(F32)  5.71 us
    unnamed x20, local copies, waits for them, and re-layouts  4.99 us
    dot_general x1, matrix products, per_device(): mix = jnp.dot(weights, out, preferred_element_type=F32).astype(BF16)  4.13 us
    dot_general x1, matrix products, per_device(): jnp.einsum('irs,ird->isd', hot.astype(BF16), both, preferred_element_type...  3.28 us
  transfers between devices with their start and end apart: 5, of which 4 were waited for; matrix products, arithmetic and copies ran while one was open for 12% of the time, Pallas kernels for 0%

profile of v3, /device:TPU:0, one launch (start us, length us, event | category | flops | bytes accessed | tf_op | source)
XLA Modules:
  0.0 137.3 jit_solution(1537165546016350454)
XLA Ops:
  0.0 0.7 broadcast_compare_fusion.1
  0.7 0.9 fusion.25
  2.7 0.7 select_reduce_fusion.2
  4.0 33.6 %shard_map.82 = bf16[16,64,2176]{2,1,0:T(8,128)(2,1)S(1)} custom-call(bf16[64,2176]{1,0:T(8,128)(2,1)S(1)} %pad_maximum_fusion.3.own), custom_call_target="tpu_custom_call" | custom-call | tf_op jit(solution)/shard_map/pallas_call | solution.py:137
  37.6 2.0 %copy-done.1 = bf16[16,64,2176]{2,1,0:T(8,128)(2,1)} copy-done((bf16[16,64,2176]{2,1,0:T(8,128)(2,1)}, bf16[16,64,2176]{2,1,0:T(8,128)(2,1)S(1)}, u32[]{:S(2)}) %copy-start.1) | copy-done | bytes 4456472
  40.1 0.8 fusion.83
  41.6 1.5 %collective-permute-start = (f32[16,64]{1,0:T(8,128)S(1)}, f32[16,64]{1,0:T(8,128)S(1)}, u32[]{:S(2)}, u32[]{:S(2)}) collective-permute-start(f32[16,64]{1,0:T(8,128)S(1)} %slice_bitcast_fusion.2), channel_id=1, source_target_pairs={{0,16},{16,0},{1,17},{17,1},{2,18},{18,2},{3,19},{19,3},{4,20},{20... | collective-permute-start | bytes 12296 | tf_op jit(solution)/shard_map/ppermute | solution.py:22
  43.2 1.2 dynamic-slice_convert_fusion
  44.9 1.0 copy.52
  46.2 1.2 broadcast_in_dim.93
  48.1 6.0 %slice_bitcast_fusion.1 = (bf16[2048,1024]{1,0:T(8,128)(2,1)}, bf16[2048,1024]{1,0:T(8,128)(2,1)}) fusion(bf16[2,2048,1024]{2,1,0:T(8,128)(2,1)} %param.14), kind=kLoop, calls=%fused_computation.9 | loop fusion | bytes 16777216 | tf_op jit(solution)/shard_map/squeeze | solution.py:323
  54.5 0.8 copy.56
  56.0 0.8 copy.54
  56.8 0.7 add_rsqrt_fusion
  58.0 3.3 %multiply_convert_fusion = bf16[16,32,2048]{2,1,0:T(8,128)(2,1)S(1)} fusion(bf16[16,64,2176]{2,1,0:T(8,128)(2,1)} %copy-done.1, f32[2048]{0:T(1024)S(1)} %copy-done.7, f32[16,32]{1,0:T(8,128)S(1)} %copy.58, pred[16,64,32]{1,2,0:T(32,128)(4,1)S(1)} %copy.56, s32[16,64,32]{1,2,0:T(8,128)S(1)} %copy.55, s32[32]{0:T(128)S(1)} %eq.132), kind=kOutput, calls=%fused_computation.10 | convolution fusion | flops 137428992 | bytes 6465664 | tf_op jit(solution)/shard_map/irs,ird->isd/dot_general | solution.py:310
  61.5 0.7 fusion.73
  62.3 0.7 fusion.74
  63.6 1.5 %collective-permute-start.1 = (bf16[256,512]{1,0:T(8,128)(2,1)S(1)}, bf16[256,512]{1,0:T(8,128)(2,1)S(1)}, u32[]{:S(2)}, u32[]{:S(2)}) collective-permute-start(bf16[256,512]{1,0:T(8,128)(2,1)S(1)} %get-tuple-element.23), channel_id=1, source_target_pairs={{0,16},{16,0},{1,17},{17,1},{2,18},{18,2},{3,19},{19,3},{4,20},{20... | collective-permute-start | bytes 786440 | tf_op jit(solution)/shard_map/ppermute | solution.py:22
  65.1 0.7 fusion.71
  65.9 0.7 fusion.72
  67.2 1.5 %collective-permute-start.3 = (bf16[256,512]{1,0:T(8,128)(2,1)S(1)}, bf16[256,512]{1,0:T(8,128)(2,1)S(1)}, u32[]{:S(2)}, u32[]{:S(2)}) collective-permute-start(bf16[256,512]{1,0:T(8,128)(2,1)S(1)} %get-tuple-element.19), channel_id=1, source_target_pairs={{0,16},{16,0},{1,17},{17,1},{2,18},{18,2},{3,19},{19,3},{4,20},{20... | collective-permute-start | bytes 786440 | tf_op jit(solution)/shard_map/ppermute | solution.py:22
  68.7 3.5 %collective-permute-done.2 = bf16[256,512]{1,0:T(8,128)(2,1)S(1)} collective-permute-done((bf16[256,512]{1,0:T(8,128)(2,1)S(1)}, bf16[256,512]{1,0:T(8,128)(2,1)S(1)}, u32[]{:S(2)}, u32[]{:S(2)}) %collective-permute-start.2) | collective-permute-done | bytes 262176 | tf_op jit(solution)/shard_map/ppermute | solution.py:22
  72.3 5.5 %collective-permute-done.1 = bf16[256,512]{1,0:T(8,128)(2,1)S(1)} collective-permute-done((bf16[256,512]{1,0:T(8,128)(2,1)S(1)}, bf16[256,512]{1,0:T(8,128)(2,1)S(1)}, u32[]{:S(2)}, u32[]{:S(2)}) %collective-permute-start.1) | collective-permute-done | bytes 262176 | tf_op jit(solution)/shard_map/ppermute | solution.py:22
  78.0 1.3 fusion.10
  79.3 4.2 %collective-permute-done.4 = bf16[256,512]{1,0:T(8,128)(2,1)S(1)} collective-permute-done((bf16[256,512]{1,0:T(8,128)(2,1)S(1)}, bf16[256,512]{1,0:T(8,128)(2,1)S(1)}, u32[]{:S(2)}, u32[]{:S(2)}) %collective-permute-start.4) | collective-permute-done | bytes 262176 | tf_op jit(solution)/shard_map/ppermute | solution.py:22
  83.5 4.7 %collective-permute-done.3 = bf16[256,512]{1,0:T(8,128)(2,1)S(1)} collective-permute-done((bf16[256,512]{1,0:T(8,128)(2,1)S(1)}, bf16[256,512]{1,0:T(8,128)(2,1)S(1)}, u32[]{:S(2)}, u32[]{:S(2)}) %collective-permute-start.3) | collective-permute-done | bytes 262176 | tf_op jit(solution)/shard_map/ppermute | solution.py:22
  88.3 1.3 fusion.13
  89.8 0.7 copy-done.6
  90.6 4.1 %convolution_convert_fusion = bf16[1024,2048]{1,0:T(8,128)(2,1)} fusion(bf16[512,2048]{1,0:T(8,128)(2,1)S(1)} %bitcast.67, bf16[1024,32]{1,0:T(8,128)(2,1)S(1)} %bitcast.74, s32[512]{0:T(512)S(1)} %get-tuple-element.26, s32[1024]{0:T(1024)S(1)} %add_select_fusion, s32[512]{0:T(512)S(1)} %get-tuple-element.25), kind=kOutput, calls=%fused_computation.11 | convolution fusion | flops 2184724480 | bytes 6365184 | tf_op jit(solution)/shard_map/dot_general | solution.py:342
  94.7 2.2 %copy-done.2 = bf16[1024,2048]{1,0:T(8,128)(2,1)S(1)} copy-done((bf16[1024,2048]{1,0:T(8,128)(2,1)S(1)}, bf16[1024,2048]{1,0:T(8,128)(2,1)}, u32[]{:S(2)}) %copy-start.2) | copy-done | bytes 4194328
  96.9 39.5 %shard_map.83 = f32[64,2048]{1,0:T(8,128)S(1)} custom-call(bf16[16,64,2048]{2,1,0:T(8,128)(2,1)S(1)} %bitcast.59), custom_call_target="tpu_custom_call" | custom-call | tf_op jit(solution)/shard_map/pallas_call | solution.py:238
  136.4 0.9 add.101
  (58 shorter events, 7.7 us)
Async XLA Ops:
  0.0 2.3 %copy-start = (bf16[128,2048]{1,0:T(8,128)(2,1)S(1)}, bf16[128,2048]{1,0:T(8,128)(2,1)}, u32[]{:S(2)}) copy-start(bf16[128,2048]{1,0:T(8,128)(2,1)} %param.8) | copy-start | bytes 1572868
  37.6 2.0 %copy-start.1 = (bf16[16,64,2176]{2,1,0:T(8,128)(2,1)}, bf16[16,64,2176]{2,1,0:T(8,128)(2,1)S(1)}, u32[]{:S(2)}) copy-start(bf16[16,64,2176]{2,1,0:T(8,128)(2,1)S(1)} %shard_map.82) | copy-start | bytes 13369348
  41.6 15.3 %collective-permute-start = (f32[16,64]{1,0:T(8,128)S(1)}, f32[16,64]{1,0:T(8,128)S(1)}, u32[]{:S(2)}, u32[]{:S(2)}) collective-permute-start(f32[16,64]{1,0:T(8,128)S(1)} %slice_bitcast_fusion.2), channel_id=1, source_target_pairs={{0,16},{16,0},{1,17},{17,1},{2,18},{18,2},{3,19},{19,3},{4,20},{20... | collective-permute-start | bytes 12296 | tf_op jit(solution)/shard_map/ppermute | solution.py:22
  48.1 6.0 %copy-start.5 = (pred[16,16,4,32]{3,0,2,1:T(8,128)(4,1)S(1)}, pred[16,16,4,32]{3,0,2,1:T(8,128)(4,1)}, u32[]{:S(2)}) copy-start(pred[16,16,4,32]{3,0,2,1:T(8,128)(4,1)} %copy.52) | copy-start | bytes 98308
  54.1 3.9 %copy-start.7 = (f32[2048]{0:T(1024)S(1)}, f32[2048]{0:T(1024)}, u32[]{:S(2)}) copy-start(f32[2048]{0:T(1024)} %param.9) | copy-start | bytes 24580
  58.0 3.5 %copy-start.4 = (bf16[2048,1024]{1,0:T(8,128)(2,1)S(1)}, bf16[2048,1024]{1,0:T(8,128)(2,1)}, u32[]{:S(2)}) copy-start(bf16[2048,1024]{1,0:T(8,128)(2,1)} %get-tuple-element.8) | copy-start | bytes 12582916
  61.5 3.6 %copy-start.3 = (bf16[2048,1024]{1,0:T(8,128)(2,1)S(1)}, bf16[2048,1024]{1,0:T(8,128)(2,1)}, u32[]{:S(2)}) copy-start(bf16[2048,1024]{1,0:T(8,128)(2,1)} %get-tuple-element.9) | copy-start | bytes 12582916
  62.2 15.7 %slice-start = ((s8[8388608]{0:T(1024)(128)(4,1)}), s8[4194304]{0:T(1024)(128)(4,1)S(1)}, s32[]{:S(2)}) async-start(s8[8388608]{0:T(1024)(128)(4,1)} %bitcast.77), calls=%async_computation | async-start | bytes 8388608
  63.0 9.2 %collective-permute-start.2 = (bf16[256,512]{1,0:T(8,128)(2,1)S(1)}, bf16[256,512]{1,0:T(8,128)(2,1)S(1)}, u32[]{:S(2)}, u32[]{:S(2)}) collective-permute-start(bf16[256,512]{1,0:T(8,128)(2,1)S(1)} %get-tuple-element.21), channel_id=1, source_target_pairs={{0,16},{16,0},{1,17},{17,1},{2,18},{18,2},{3,19},{19,3},{4,20},{20... | collective-permute-start | bytes 786440 | tf_op jit(solution)/shard_map/ppermute | solution.py:22
  63.6 14.3 %collective-permute-start.1 = (bf16[256,512]{1,0:T(8,128)(2,1)S(1)}, bf16[256,512]{1,0:T(8,128)(2,1)S(1)}, u32[]{:S(2)}, u32[]{:S(2)}) collective-permute-start(bf16[256,512]{1,0:T(8,128)(2,1)S(1)} %get-tuple-element.23), channel_id=1, source_target_pairs={{0,16},{16,0},{1,17},{17,1},{2,18},{18,2},{3,19},{19,3},{4,20},{20... | collective-permute-start | bytes 786440 | tf_op jit(solution)/shard_map/ppermute | solution.py:22
  65.1 12.8 %slice-start.1 = ((s8[8388608]{0:T(1024)(128)(4,1)}), s8[4194304]{0:T(1024)(128)(4,1)S(1)}, s32[]{:S(2)}) async-start(s8[8388608]{0:T(1024)(128)(4,1)} %bitcast.77), calls=%async_computation.1 | async-start | bytes 8388608
  66.6 16.9 %collective-permute-start.4 = (bf16[256,512]{1,0:T(8,128)(2,1)S(1)}, bf16[256,512]{1,0:T(8,128)(2,1)S(1)}, u32[]{:S(2)}, u32[]{:S(2)}) collective-permute-start(bf16[256,512]{1,0:T(8,128)(2,1)S(1)} %get-tuple-element.17), channel_id=1, source_target_pairs={{0,16},{16,0},{1,17},{17,1},{2,18},{18,2},{3,19},{19,3},{4,20},{20... | collective-permute-start | bytes 786440 | tf_op jit(solution)/shard_map/ppermute | solution.py:22
  67.2 21.0 %collective-permute-start.3 = (bf16[256,512]{1,0:T(8,128)(2,1)S(1)}, bf16[256,512]{1,0:T(8,128)(2,1)S(1)}, u32[]{:S(2)}, u32[]{:S(2)}) collective-permute-start(bf16[256,512]{1,0:T(8,128)(2,1)S(1)} %get-tuple-element.19), channel_id=1, source_target_pairs={{0,16},{16,0},{1,17},{17,1},{2,18},{18,2},{3,19},{19,3},{4,20},{20... | collective-permute-start | bytes 786440 | tf_op jit(solution)/shard_map/ppermute | solution.py:22
  89.6 1.0 copy-start.6
  94.7 2.2 %copy-start.2 = (bf16[1024,2048]{1,0:T(8,128)(2,1)S(1)}, bf16[1024,2048]{1,0:T(8,128)(2,1)}, u32[]{:S(2)}) copy-start(bf16[1024,2048]{1,0:T(8,128)(2,1)} %convolution_convert_fusion) | copy-start | bytes 12582916
